TPU v7x, 128 devices: a whole 4x4x4 slice. The times are simulated.
128 devices in a mesh: ctx: 8 (over y, x_hi), dp: 16 (over x_lo, z, core).
Axes of the slice: x: 4 (x_hi: 2, x_lo: 2; x = x_hi * 2 + x_lo), y: 4, z: 4, core: 2. Of those that a mesh axis runs over, the one named last changes fastest.
Arguments:
- events: bfloat16 [16, 4096, 512], P('dp', 'ctx'), may hold values from -6 to 6
- lengths: int32 [16, 4], P('dp'), may hold values from 1 to 3072, 4096 in all within a row
- target_rows: int32 [16, 1024], P('dp', 'ctx'), may hold values from 0 to 511, as said below
- position_ids: int32 [16, 1024], P('dp', 'ctx'), may hold values from 0 to 255
- labels: int32 [16, 1024], P('dp', 'ctx'), may hold values 0 or 1
- upstream: bfloat16 [16, 4096, 512], P('dp', 'ctx'), may hold values from -0.059814453 to 0.059814453
- w_in: bfloat16 [512, 2048], P(('ctx', 'dp')), may hold values from -0.25 to 0.25
- w_out: bfloat16 [512, 512], P(('ctx', 'dp')), may hold values from -0.25 to 0.25
- head_w1: bfloat16 [512, 256], replicated, may hold values from -0.25 to 0.25
- head_w2: float32 [256], replicated, may hold values from -0.375 to 0.375
- table: float32 [256, 128], replicated, may hold values from -6 to 6
- bias_w1: float32 [128, 128], replicated, may hold values from -0.5 to 0.5
- bias_w2: float32 [128], replicated, may hold values from -0.5 to 0.5
Outputs:
- grad_w_in: float32 [512, 2048], P(('ctx', 'dp'))
- grad_w_out: float32 [512, 512], P(('ctx', 'dp'))
- grad_head_w1: float32 [512, 256], P(('ctx', 'dp'))
- grad_head_w2: float32 [256], P(('ctx', 'dp'))
- grad_table: float32 [256, 128], P(('ctx', 'dp'))
- grad_bias_w1: float32 [128, 128], P(('ctx', 'dp'))
- grad_bias_w2: float32 [128], P(('ctx', 'dp'))
Inputs may be any that keep to these rules, and one draw needn't show every extreme that they name: Each group's 4 lengths sum to 4096. `target_rows`: the 128 entries of one device are distinct.
All inputs are finite; a program needn't handle non-finite values. No bound on the sum of `labels` on one device may be relied on, other than what follows from the above.
Results may differ from a plain program's by a relative error of at most 0.0095.
Values may be sent and summed in bfloat16 or wider, within the bound.
No kernel may reach another device: no remote copies, remote signals or barrier semaphores. Data moves between devices by JAX's collectives and lax.ppermute only.
A program may use at most 192 MiB of HBM per device.

v0:
```python
import math

import jax
import jax.numpy as jnp
from jax import lax
from jax.sharding import PartitionSpec as P

HEADS = 4


EPSILON = 1e-05
HIGHEST = lax.Precision.HIGHEST


def normalize(matrix):
    average = jnp.mean(matrix, axis=-1, keepdims=True)
    centred = matrix - average
    inverse = lax.rsqrt(jnp.mean(centred * centred, axis=-1, keepdims=True) + EPSILON)
    return (centred * inverse, inverse)


def normalize_back(upward, normed, inverse):
    first = jnp.mean(upward, axis=-1, keepdims=True)
    second = jnp.mean(upward * normed, axis=-1, keepdims=True)
    return inverse * (upward - first - normed * second)


def silu_slope(argument):
    sigmoid_value = jax.nn.sigmoid(argument)
    return sigmoid_value * (1.0 + argument * (1.0 - sigmoid_value))


def document(positions, user_lengths):
    user_ends = jnp.cumsum(user_lengths)
    return jnp.sum(
        (positions[:, None] >= user_ends[None, :]).astype(jnp.int32), axis=1, dtype=jnp.int32
    )


def block_weights(query3, query_pos, query_doc, key3, key_pos, key_doc, score_scale):
    allowed = (query_doc[:, None] == key_doc[None, :]) & (key_pos[None, :] <= query_pos[:, None])
    scores = (
        jnp.einsum("rhe,che->hrc", query3, key3, preferred_element_type=jnp.float32) * score_scale
    )
    weights = jnp.where(allowed[None], jax.nn.silu(scores), 0.0).astype(jnp.bfloat16)
    return (allowed, scores, weights)


def block_slopes(allowed, scores, grad3, value3, score_scale):
    products = jnp.einsum("rhe,che->hrc", grad3, value3, preferred_element_type=jnp.float32)
    return (jnp.where(allowed[None], products * silu_slope(scores), 0.0) * score_scale).astype(
        jnp.bfloat16
    )


def head_pass(picked, position_ids, labels, head_w1, head_w2, table, bias_w1, bias_w2):
    hidden = jnp.dot(picked, head_w1, preferred_element_type=jnp.float32)
    active = jax.nn.silu(hidden)
    relevance = jnp.dot(active, head_w2, precision=HIGHEST)
    slots = jnp.arange(table.shape[0], dtype=jnp.int32)
    selector = (position_ids[:, None] == slots[None, :]).astype(jnp.float32)
    embedded = jnp.dot(selector, table, precision=HIGHEST)
    bias_pre = jnp.dot(embedded, bias_w1, precision=HIGHEST)
    bias_hidden = jax.nn.silu(bias_pre)
    observe = jnp.dot(bias_hidden, bias_w2, precision=HIGHEST)
    rel_sig = jax.nn.sigmoid(relevance)
    obs_sig = jax.nn.sigmoid(observe)
    missing = jax.nn.sigmoid(-relevance) + rel_sig * jax.nn.sigmoid(-observe)
    clicked = labels.astype(jnp.float32)
    d_relevance = (
        clicked * (rel_sig - 1.0) + (1.0 - clicked) * rel_sig * (1.0 - rel_sig) * obs_sig / missing
    )
    d_observe = (
        clicked * (obs_sig - 1.0) + (1.0 - clicked) * rel_sig * obs_sig * (1.0 - obs_sig) / missing
    )
    d_hidden = (d_relevance[:, None] * head_w2[None, :] * silu_slope(hidden)).astype(jnp.bfloat16)
    grad_h1 = lax.dot_general(
        picked, d_hidden, (((0,), (0,)), ((), ())), preferred_element_type=jnp.float32
    )
    grad_h2 = jnp.dot(d_relevance, active, precision=HIGHEST)
    d_bias = d_observe[:, None] * bias_w2[None, :] * silu_slope(bias_pre)
    grad_b1 = jnp.dot(embedded.T, d_bias, precision=HIGHEST)
    grad_b2 = jnp.dot(d_observe, bias_hidden, precision=HIGHEST)
    d_embedded = jnp.dot(d_bias, bias_w1.T, precision=HIGHEST)
    grad_tab = jnp.dot(selector.T, d_embedded, precision=HIGHEST)
    d_picked = lax.dot_general(
        d_hidden, head_w1, (((1,), (1,)), ((), ())), preferred_element_type=jnp.float32
    ).astype(jnp.bfloat16)
    return (grad_h1, grad_h2, grad_tab, grad_b1, grad_b2, d_picked)


def body(
    events,
    lengths,
    target_rows,
    position_ids,
    labels,
    upstream,
    w_in,
    w_out,
    head_w1,
    head_w2,
    table,
    bias_w1,
    bias_w2,
):
    local_events = events[0]
    rows_here, feature_width = local_events.shape
    head_size = feature_width // HEADS
    score_scale = 1.0 / math.sqrt(head_size)
    user_lengths = lengths[0]
    contexts = lax.axis_size("ctx")
    row_base = lax.axis_index("ctx") * rows_here
    w_in_full, w_out_full = (
        lax.all_gather(w_in, ("ctx", "dp"), axis=0, tiled=True),
        lax.all_gather(w_out, ("ctx", "dp"), axis=0, tiled=True),
    )
    normed, _ = normalize(local_events.astype(jnp.float32))
    normed = normed.astype(jnp.bfloat16)
    preact = jnp.dot(normed, w_in_full, preferred_element_type=jnp.float32)
    projected = jax.nn.silu(preact).astype(jnp.bfloat16)
    gate_rows = projected[:, :feature_width].astype(jnp.float32)
    value_rows = projected[:, feature_width : 2 * feature_width]
    query_rows = projected[:, 2 * feature_width : 3 * feature_width]
    key_rows = projected[:, 3 * feature_width :]
    local_pos = row_base + jnp.arange(rows_here, dtype=jnp.int32)
    local_doc = document(local_pos, user_lengths)
    query3 = query_rows.reshape(rows_here, HEADS, head_size)
    sent_rows = (key_rows, value_rows)

    def key_pair(shard_piece):
        return (shard_piece[0], shard_piece[1])

    zero_rows = jnp.zeros((rows_here, feature_width), jnp.float32)
    keys_all, values_all = key_pair(
        (
            lax.all_gather(sent_rows[0], "ctx", axis=0, tiled=True),
            lax.all_gather(sent_rows[1], "ctx", axis=0, tiled=True),
        )
    )
    piece_rows = keys_all.shape[0]
    step_rows = math.gcd(piece_rows, 512)

    def forward_advance(block_turn, partial_value):
        offset = block_turn * step_rows
        key3 = lax.dynamic_slice_in_dim(keys_all, offset, step_rows, 0).reshape(
            step_rows, HEADS, head_size
        )
        value3 = lax.dynamic_slice_in_dim(values_all, offset, step_rows, 0).reshape(
            step_rows, HEADS, head_size
        )
        key_pos = offset + jnp.arange(step_rows, dtype=jnp.int32)
        _, _, weights = block_weights(
            query3,
            local_pos,
            local_doc,
            key3,
            key_pos,
            document(key_pos, user_lengths),
            score_scale,
        )
        return partial_value + jnp.einsum(
            "hrc,che->rhe", weights, value3, preferred_element_type=jnp.float32
        ).reshape(rows_here, feature_width)

    attended = lax.fori_loop(0, piece_rows // step_rows, forward_advance, zero_rows)
    attn_norm, inverse = normalize(attended)
    gated = (attn_norm * gate_rows).astype(jnp.bfloat16)
    layer_out = (
        jnp.dot(gated, w_out_full, preferred_element_type=jnp.float32)
        + local_events.astype(jnp.float32)
    ).astype(jnp.bfloat16)
    placing = (jnp.arange(rows_here, dtype=jnp.int32)[:, None] == target_rows[0][None, :]).astype(
        jnp.bfloat16
    )
    picked = lax.dot_general(
        placing, layer_out, (((0,), (0,)), ((), ())), preferred_element_type=jnp.float32
    ).astype(jnp.bfloat16)
    grad_h1, grad_h2, grad_tab, grad_b1, grad_b2, d_picked = head_pass(
        picked, position_ids[0], labels[0], head_w1, head_w2, table, bias_w1, bias_w2
    )
    d_out = (
        upstream[0].astype(jnp.float32)
        + jnp.dot(placing, d_picked, preferred_element_type=jnp.float32)
    ).astype(jnp.bfloat16)
    grad_wo = lax.dot_general(
        gated, d_out, (((0,), (0,)), ((), ())), preferred_element_type=jnp.float32
    )
    d_gated = lax.dot_general(
        d_out, w_out_full, (((1,), (1,)), ((), ())), preferred_element_type=jnp.float32
    )
    d_gate = d_gated * attn_norm
    d_attended = normalize_back(d_gated * gate_rows, attn_norm, inverse).astype(jnp.bfloat16)
    grad3 = d_attended.reshape(rows_here, HEADS, head_size)

    def key_terms(keys_all, values_all, offset, step_rows):
        key3 = lax.dynamic_slice_in_dim(keys_all, offset, step_rows, 0).reshape(
            step_rows, HEADS, head_size
        )
        value3 = lax.dynamic_slice_in_dim(values_all, offset, step_rows, 0).reshape(
            step_rows, HEADS, head_size
        )
        key_pos = offset + jnp.arange(step_rows, dtype=jnp.int32)
        allowed, scores, weights = block_weights(
            query3,
            local_pos,
            local_doc,
            key3,
            key_pos,
            document(key_pos, user_lengths),
            score_scale,
        )
        slopes = block_slopes(allowed, scores, grad3, value3, score_scale)
        return (key3, weights, slopes)

    back_start = (zero_rows, jnp.zeros((rows_here * contexts, 2 * feature_width), jnp.float32))
    spread_keys_all, spread_values_all = key_pair(
        (
            lax.all_gather(sent_rows[0], "ctx", axis=0, tiled=True),
            lax.all_gather(sent_rows[1], "ctx", axis=0, tiled=True),
        )
    )
    piece_rows = spread_keys_all.shape[0]
    spread_step_rows = math.gcd(piece_rows, 512)

    def spread_advance(block_turn, partial_value):
        grad_query, spread = partial_value
        offset = block_turn * spread_step_rows
        key3, weights, slopes = key_terms(
            spread_keys_all, spread_values_all, offset, spread_step_rows
        )
        grad_query = grad_query + jnp.einsum(
            "hrc,che->rhe", slopes, key3, preferred_element_type=jnp.float32
        ).reshape(rows_here, feature_width)
        grad_key = jnp.einsum(
            "hrc,rhe->che", slopes, query3, preferred_element_type=jnp.float32
        ).reshape(spread_step_rows, feature_width)
        grad_value = jnp.einsum(
            "hrc,rhe->che", weights, grad3, preferred_element_type=jnp.float32
        ).reshape(spread_step_rows, feature_width)
        former = lax.dynamic_slice_in_dim(spread, offset, spread_step_rows, 0)
        spread = lax.dynamic_update_slice_in_dim(
            spread, former + jnp.concatenate([grad_key, grad_value], axis=1), offset, 0
        )
        return (grad_query, spread)

    folded = lax.fori_loop(0, piece_rows // spread_step_rows, spread_advance, back_start)
    grad_query, spread = folded
    summed = lax.psum_scatter(
        spread.astype(jnp.bfloat16), "ctx", scatter_dimension=0, tiled=True
    ).astype(jnp.float32)
    grad_keys = summed[:, :feature_width]
    grad_values = summed[:, feature_width:]
    d_projected = jnp.concatenate([d_gate, grad_values, grad_query, grad_keys], axis=1)
    d_preact = (d_projected * silu_slope(preact)).astype(jnp.bfloat16)
    grad_wi = lax.dot_general(
        normed, d_preact, (((0,), (0,)), ((), ())), preferred_element_type=jnp.float32
    )
    totals = (
        lax.psum_scatter(grad_wi, ("ctx", "dp"), scatter_dimension=0, tiled=True),
        lax.psum_scatter(grad_wo, ("ctx", "dp"), scatter_dimension=0, tiled=True),
        lax.psum_scatter(grad_h1, ("ctx", "dp"), scatter_dimension=0, tiled=True),
        lax.psum_scatter(grad_h2, ("ctx", "dp"), scatter_dimension=0, tiled=True),
        lax.psum_scatter(grad_tab, ("ctx", "dp"), scatter_dimension=0, tiled=True),
        lax.psum_scatter(grad_b1, ("ctx", "dp"), scatter_dimension=0, tiled=True),
        lax.psum_scatter(grad_b2, ("ctx", "dp"), scatter_dimension=0, tiled=True),
    )
    return (totals[0], totals[1], totals[2], totals[3], totals[4], totals[5], totals[6])


def solution(mesh):
    in_specs = (
        P("dp", "ctx", None),
        P("dp", None),
        P("dp", "ctx"),
        P("dp", "ctx"),
        P("dp", "ctx"),
        P("dp", "ctx", None),
        P(("ctx", "dp"), None),
        P(("ctx", "dp"), None),
        P(),
        P(),
        P(),
        P(),
        P(),
    )
    out_specs = (
        P(("ctx", "dp"), None),
        P(("ctx", "dp"), None),
        P(("ctx", "dp"), None),
        P(("ctx", "dp")),
        P(("ctx", "dp"), None),
        P(("ctx", "dp"), None),
        P(("ctx", "dp")),
    )
    return jax.shard_map(body, mesh=mesh, in_specs=in_specs, out_specs=out_specs, check_vma=False)
```

profile of v0, /device:TPU:0, one launch (start us, length us, event | category | flops | bytes accessed | tf_op | source)
XLA Modules:
  0.0 900.0 jit_solution(5169362681839176217)
XLA Ops:
  10.5 68.4 %all-gather.10.cloned.1.call-done = bf16[128,4,2048]{2,1,0:T(4,128)(2,1)} async-done(((bf16[1,4,2048]{2,1,0:T(4,128)(2,1)}), bf16[128,4,2048]{2,1,0:T(4,128)(2,1)}) %all-gather.10.cloned.1.call-update) | async-done | bytes 2097168 | tf_op jit(solution)/shard_map/all_gather | solution.py:115
  89.0 34.4 %all-gather.1 = bf16[128,4,512]{2,1,0:T(4,128)(2,1)S(1)} all-gather(bf16[1,4,512]{2,1,0:T(4,128)(2,1)S(1)} %bitcast.236), channel_id=1, replica_groups=mesh['ctx'=8,'dp'=16] {'ctx','dp'}, dimensions={0}, use_global_device_ids=true | all-gather | bytes 528384 | tf_op jit(solution)/shard_map/all_gather | solution.py:116
  126.7 30.4 %all-gather.8.cloned.1.call-done = bf16[4096,512]{1,0:T(8,128)(2,1)} async-done(((bf16[512,512]{1,0:T(8,128)(2,1)}), bf16[4096,512]{1,0:T(8,128)(2,1)}) %all-gather.8.cloned.1.call-update) | async-done | bytes 4194320 | tf_op jit(solution)/shard_map/all_gather | solution.py:137
  157.1 6.4 copy.100
  163.5 65.2 %all-gather.6.cloned.1.call-done = bf16[4096,512]{1,0:T(8,128)(2,1)} async-done(((bf16[512,512]{1,0:T(8,128)(2,1)}), bf16[4096,512]{1,0:T(8,128)(2,1)}) %all-gather.6.cloned.1.call-update) | async-done | bytes 4194320 | tf_op jit(solution)/shard_map/all_gather | solution.py:138
  228.7 6.4 copy.99
  235.1 52.5 %while.34 = (s32[]{:T(128)}, f32[512,512]{0,1:T(8,128)S(1)}, bf16[4096,512]{0,1:T(8,128)(2,1)}, s32[512]{0:T(512)S(1)}, s32[1,4]{1,0:T(1,128)S(1)}, /*index=5*/b...) while((s32[]{:T(128)}, f32[512,512]{0,1:T(8,128)S(1)}, ...), condition=%wide.region_7.8_spmd.clone, body=%wide.region_5.7_spmd.clone.sunk | while | flops 545528320 | bytes 8405201 | solution.py:166
  300.2 7.9 broadcast_in_dim.131.clone
  308.1 291.9 %while.35 = (s32[]{:T(128)}, f32[512,512]{0,1:T(8,128)}, f32[4096,1024]{1,0:T(8,128)}, bf16[4096,512]{0,1:T(8,128)(2,1)}, s32[512]{0:T(512)S(1)}, /*index=5*/s32...) while((s32[]{:T(128)}, f32[512,512]{0,1:T(8,128)}, ...), condition=%wide.region_14.15_spmd.clone, body=%wide.region_12.14_spmd.clone.sunk | while | flops 1364466176 | bytes 84689256 | solution.py:247
  309.6 4.9 fusion.144
  314.5 5.3 copy.140
  345.0 4.9 fusion.144
  350.0 5.3 copy.140
  381.6 4.9 fusion.144
  386.6 5.3 copy.140
  418.3 4.9 fusion.144
  423.2 5.3 copy.140
  455.0 4.9 fusion.144
  459.9 5.3 copy.140
  479.4 3.7 fusion.147
  491.6 4.9 fusion.144
  496.6 5.3 copy.140
  516.0 3.7 fusion.147
  528.3 4.9 fusion.144
  533.2 5.3 copy.140
  564.9 4.9 fusion.144
  569.8 5.3 copy.140
  600.0 9.2 %convert_element_type.125 = bf16[4096,1024]{1,0:T(8,128)(2,1)} convert(f32[4096,1024]{1,0:T(8,128)} %get-tuple-element.433) | non-fusion elementwise | flops 4194304 | bytes 25165824 | tf_op jit(solution)/shard_map/convert_element_type | solution.py:250
  618.1 103.4 %reduce-scatter.2.cloned.1.call-done = bf16[512,1024]{1,0:T(8,128)(2,1)} async-done(((bf16[4096,1024]{1,0:T(8,128)(2,1)}), bf16[512,1024]{1,0:T(8,128)(2,1)}) %reduce-scatter.2.cloned.1.call-update) | async-done | bytes 1048592 | tf_op jit(solution)/shard_map/reduce_scatter | solution.py:249
  723.0 6.4 fusion.29
  730.6 64.3 %all-reduce.7 = (f32[256]{0:T(256)S(1)}, f32[128]{0:T(128)S(1)}) all-reduce(f32[256]{0:T(256)S(1)} %bitcast.244, f32[128]{0:T(128)S(1)} %convolution_bitcast_fusion), channel_id=6, replica_groups=mesh['ctx'=8,'dp'=16] {'ctx','dp'}, use_global_device_ids=true, to_apply=%region_19.20.clone | all-reduce | flops 384 | bytes 3072
  796.1 90.9 %all-reduce.11.cloned.1.call-done = (f32[512,2048]{1,0:T(8,128)}, f32[512,512]{1,0:T(8,128)}, f32[512,256]{1,0:T(8,128)}, f32[256,128]{1,0:T(8,128)}, f32[128,128]{1,0:T(8,128)}) async-done(((f32[512,2048]{1,0:T(8,128)}, f32[512,512]{1,0:T(8,128)}, f32[512,256]{1,0:T(8,128)}, f32[256,128]{1,0:T(8,128)}, f32[128,128]{1,0:T(8,128)}), (f32[512,2048]{1,0:T(8,128)}, f32[512,512]{1,0:T(8,128)}, ...) | async-done | bytes 5963792
  (382 shorter events, 302.4 us)
Async XLA Ops:
  7.2 284.4 %copy-start = (bf16[512,256]{1,0:T(8,128)(2,1)S(1)}, bf16[512,256]{1,0:T(8,128)(2,1)}, u32[]{:S(2)}) copy-start(bf16[512,256]{1,0:T(8,128)(2,1)} %param.25) | copy-start | bytes 786436
  7.2 74.3 %copy-start.10 = (bf16[1,512,512]{2,1,0:T(8,128)(2,1)S(1)}, bf16[1,512,512]{2,1,0:T(8,128)(2,1)}, u32[]{:S(2)}) copy-start(bf16[1,512,512]{2,1,0:T(8,128)(2,1)} %param.17) | copy-start | bytes 1572868
  7.2 71.8 %all-gather.10.cloned.1.call-start = ((), (), s32[]{:S(2)}) async-start(), calls=%async_computation.4 | async-start | bytes 2113536 | tf_op jit(solution)/shard_map/all_gather | solution.py:115
  7.9 149.2 %all-gather.8.cloned.1.call-start = ((), (), s32[]{:S(2)}) async-start(), calls=%async_computation.2 | async-start | bytes 4718592 | tf_op jit(solution)/shard_map/all_gather | solution.py:137
  9.2 72.3 %copy-start.28 = (f32[512]{0:T(512)}, f32[512]{0:T(512)S(1)}, u32[]{:S(2)}) copy-start(f32[512]{0:T(512)S(1)} %broadcast_multiply_fusion.3) | copy-start | bytes 6148
  10.5 71.0 %copy-start.33 = (f32[512]{0:T(512)}, f32[512]{0:T(512)S(1)}, u32[]{:S(2)}) copy-start(f32[512]{0:T(512)S(1)} %add_rsqrt_fusion.1) | copy-start | bytes 6148
  85.2 39.3 %copy-start.19 = (f32[256,128]{1,0:T(8,128)S(1)}, f32[256,128]{1,0:T(8,128)}, u32[]{:S(2)}) copy-start(f32[256,128]{1,0:T(8,128)} %param.27) | copy-start | bytes 393220
  85.2 39.3 %copy-start.31 = (s32[1,128]{1,0:T(1,128)S(1)}, s32[1,128]{1,0:T(1,128)}, u32[]{:S(2)}) copy-start(s32[1,128]{1,0:T(1,128)} %param.20) | copy-start | bytes 1540
  85.2 40.2 %copy-start.24 = (f32[128,128]{1,0:T(8,128)S(1)}, f32[128,128]{1,0:T(8,128)}, u32[]{:S(2)}) copy-start(f32[128,128]{1,0:T(8,128)} %param.28) | copy-start | bytes 196612
  87.8 140.9 %all-gather.6.cloned.1.call-start = ((), (), s32[]{:S(2)}) async-start(), calls=%async_computation.1 | async-start | bytes 4718592 | tf_op jit(solution)/shard_map/all_gather | solution.py:138
  88.6 632.9 %reduce-scatter.2.cloned.1.call-start = ((), (), s32[]{:S(2)}) async-start(), calls=%async_computation.3 | async-start | bytes 9437184 | tf_op jit(solution)/shard_map/reduce_scatter | solution.py:249
  125.6 166.5 %copy-start.26 = (f32[128,128]{1,0:T(8,128)}, f32[128,128]{1,0:T(8,128)S(1)}, u32[]{:S(2)}) copy-start(f32[128,128]{1,0:T(8,128)S(1)} %fusion.79) | copy-start | bytes 196612
  308.1 6.4 copy-start.5
  343.6 6.4 copy-start.5
  380.1 6.4 copy-start.5
  416.8 6.4 copy-start.5
  453.5 6.4 copy-start.5
  473.2 6.1 copy-start.7
  490.1 6.4 copy-start.5
  509.9 6.1 copy-start.7
  526.8 6.4 copy-start.5
  546.5 6.1 copy-start.7
  563.4 6.4 copy-start.5
  583.1 6.1 copy-start.7
  609.2 7.4 copy-start.13
  609.2 7.4 copy-start.15
  609.2 277.7 %all-reduce.11.cloned.1.call-start = ((), (), s32[]{:S(2)}) async-start(), calls=%async_computation.5 | async-start | bytes 11927552
  610.7 112.2 %copy-start.11 = (bf16[1,512,512]{2,1,0:T(8,128)(2,1)S(1)}, bf16[1,512,512]{2,1,0:T(8,128)(2,1)}, u32[]{:S(2)}) copy-start(bf16[1,512,512]{2,1,0:T(8,128)(2,1)} %param.17) | copy-start | bytes 1572868
  610.7 112.2 %copy-start.29 = (f32[512]{0:T(512)S(1)}, f32[512]{0:T(512)}, u32[]{:S(2)}) copy-start(f32[512]{0:T(512)} %copy-done.28) | copy-start | bytes 6148
  610.7 112.2 %copy-start.34 = (f32[512]{0:T(512)S(1)}, f32[512]{0:T(512)}, u32[]{:S(2)}) copy-start(f32[512]{0:T(512)} %copy-done.33) | copy-start | bytes 6148
  618.1 104.9 %copy-start.16 = (f32[512,512]{1,0:T(8,128)S(1)}, f32[512,512]{1,0:T(8,128)}, u32[]{:S(2)}) copy-start(f32[512,512]{1,0:T(8,128)} %get-tuple-element.632) | copy-start | bytes 3145732
  723.0 170.5 %copy-start.1 = (bf16[512,256]{1,0:T(8,128)(2,1)S(1)}, bf16[512,256]{1,0:T(8,128)(2,1)}, u32[]{:S(2)}) copy-start(bf16[512,256]{1,0:T(8,128)(2,1)} %param.25) | copy-start | bytes 786436
  (51 other events, 179.4 us)
Sparse Core Ops, SparseCore 0:
  11.2 67.7 all-gather.9
  87.9 69.1 all-gather.7
  159.5 69.1 all-gather.5
  609.3 112.0 reduce-scatter.1
  729.5 157.3 all-reduce.10
where the time goes:
time: 905 us; the launch traced here: 900 us
  waiting for transfers between devices  360 us (40%)
  local copies, waits for them, and re-layouts  211 us (23%)
  matrix products  163 us (18%)
  blocking collectives  98.8 us (11%)
  other arithmetic  52.1 us (6%)
  between operations  14.3 us (2%)
    reduce_scatter x1, waiting for transfers between devices, body(): lax.psum_scatter(spread.astype(jnp.bfloat16), 'ctx', scatter_dimension=0,...  103 us
    unnamed x6, waiting for transfers between devices  92.3 us
    all_gather x1, waiting for transfers between devices, body(): lax.all_gather(w_in, ('ctx', 'dp'), axis=0, tiled=True)  68.4 us
    all_gather x1, waiting for transfers between devices, body(): lax.all_gather(sent_rows[1], 'ctx', axis=0, tiled=True)  65.2 us
    unnamed x1, blocking collectives  64.3 us
    dynamic_slice x16, local copies, waits for them, and re-layouts, spread_advance(): former = lax.dynamic_slice_in_dim(spread, offset, spread_step_rows, 0)  49.1 us
    mul x8, local copies, waits for them, and re-layouts, silu_slope(): return sigmoid_value * (1.0 + argument * (1.0 - sigmoid_value))  42.3 us
    dynamic_update_slice x16, local copies, waits for them, and re-layouts, spread_advance(): lax.dynamic_update_slice_in_dim(spread, former + jnp.concatenate([grad_ke...  40.1 us
  transfers between devices with their start and end apart: 5, of which 5 were waited for; matrix products, arithmetic and copies ran while one was open for 2% of the time, Pallas kernels for 0%

commit v1 on v0

v1 whole, which is shorter than its diff:
```python
import functools
import math

import jax
import jax.numpy as jnp
from jax import lax
from jax.experimental import pallas as pl
from jax.experimental.pallas import tpu as pltpu
from jax.sharding import Mesh, PartitionSpec as P

HEADS = 4
EPSILON = 1e-05
HIGHEST = lax.Precision.HIGHEST
F32 = jnp.float32
BF16 = jnp.bfloat16
I32 = jnp.int32
R = 512
W = 512
E = 128
T = 128
SCALE = 1.0 / math.sqrt(E)
HALF = 0.5 * SCALE

NN = (((1,), (0,)), ((), ()))
NT = (((1,), (1,)), ((), ()))
TN = (((0,), (0,)), ((), ()))


def mm(a, b, dims=NN, precision=None):
    return lax.dot_general(a, b, dims, precision=precision, preferred_element_type=F32)


def silu_parts(z):
    h = 0.5 * z
    t = jnp.tanh(h)
    a = 1.0 + t
    w = h * a
    return w, 0.5 * (a + w * (1.0 - t))


def silu(z):
    h = 0.5 * z
    return h + h * jnp.tanh(h)


def vmem(n):
    return [pl.BlockSpec(memory_space=pltpu.VMEM)] * n


def smem():
    return [pl.BlockSpec(memory_space=pltpu.SMEM)]


def call(kernel, outs, args, scratch=(), limit=40, flops=0, n_smem=1, name=None):
    total = sum(a.size * a.dtype.itemsize for a in args) + sum(
        math.prod(o.shape) * o.dtype.itemsize for o in outs
    )
    return pl.pallas_call(
        kernel,
        out_shape=tuple(outs),
        in_specs=smem() * n_smem + vmem(len(args) - n_smem),
        out_specs=tuple(vmem(len(outs))),
        scratch_shapes=list(scratch),
        compiler_params=pltpu.CompilerParams(vmem_limit_bytes=limit << 20),
        cost_estimate=pl.CostEstimate(flops=flops, bytes_accessed=total, transcendentals=0),
        name=name,
    )(*args)


def sds(shape, dtype):
    return jax.ShapeDtypeStruct(shape, dtype)


def norm_kernel(x_ref, o_ref):
    x = x_ref[...].astype(F32)
    mean = jnp.mean(x, axis=-1, keepdims=True)
    cen = x - mean
    inv = lax.rsqrt(jnp.mean(cen * cen, axis=-1, keepdims=True) + EPSILON)
    o_ref[...] = (cen * inv).astype(BF16)


def user_start(pos, meta):
    start = jnp.zeros_like(pos)
    end = 0
    for j in range(3):
        end = end + meta[2 + j]
        start = jnp.where(pos >= end, end, start)
    return start


def forward_kernel(meta, n0, n1, n3, n2a, n2b, o0, o1, o3, o2a, o2b, wg, a0, a1, a2, a3, q_s, k_s, v_s):
    y, core = meta[0], meta[1]
    own = ((0, (n0,)), (1, (n1,)), (3, (n3,)), (2, (n2a, n2b)))
    oth = ((0, (o0,)), (1, (o1,)), (3, (o3,)), (2, (o2a, o2b)))
    for k, refs in own:
        blk = (y + 4 - k) & 3
        b = 2 * blk + core
        at = 0
        for ref in refs:
            n = ref.shape[0]
            p = silu(mm(ref[...], wg[:, : 3 * E])).astype(BF16)
            q_s[blk, at : at + n] = p[:, :E]
            k_s[b, at : at + n] = p[:, E : 2 * E]
            v_s[b, at : at + n] = p[:, 2 * E :]
            at += n
    for k, refs in oth:
        b = 2 * ((y + 4 - k) & 3) + 1 - core
        at = 0
        for ref in refs:
            n = ref.shape[0]
            p = silu(mm(ref[...], wg[:, E : 3 * E])).astype(BF16)
            k_s[b, at : at + n] = p[:, :E]
            v_s[b, at : at + n] = p[:, E:]
            at += n
    rows = lax.broadcasted_iota(I32, (R, 1), 0)
    lanes = lax.broadcasted_iota(I32, (1, R), 1)
    for k, out in enumerate((a0, a1, a2, a3)):
        blk = (y + k) & 3
        c = 2 * blk + core
        q = q_s[blk]
        pos = rows + c * R
        start = user_start(pos, meta)

        def step(b, acc):
            key_pos = lanes + b * R
            h = mm(q, k_s[b], NT) * HALF
            w = h + h * jnp.tanh(h)
            w = jnp.where((key_pos >= start) & (key_pos <= pos), w, 0.0).astype(BF16)
            return acc + mm(w, v_s[b])

        lo = user_start(c * R, meta) // R
        out[...] = lax.fori_loop(lo, c + 1, step, jnp.zeros((R, E), F32)).astype(BF16)


def side_kernel(
    meta, n0, n1, n3, n2a, n2b, o0, o1, o3, o2a, o2b, wg, wo_half, events, ints, table, bias_w1, bias_w2,
    sq, sk, sv, nt, u, su, w_out, ev_t, emb, bpre, obs,
):
    y, core = meta[0], meta[1]
    own = ((0, (n0,)), (1, (n1,)), (3, (n3,)), (2, (n2a, n2b)))
    oth = ((0, (o0,)), (1, (o1,)), (3, (o3,)), (2, (o2a, o2b)))
    for k, refs in own:
        blk = (y + 4 - k) & 3
        b = 2 * blk + core
        at = 0
        for ref in refs:
            n = ref.shape[0]
            x = ref[...]
            _, s = silu_parts(mm(x, wg[:, : 3 * E]))
            s = s.astype(BF16)
            sq[blk, at : at + n] = s[:, :E]
            sk[b, at : at + n] = s[:, E : 2 * E]
            sv[b, at : at + n] = s[:, 2 * E :]
            nt[b, :, at : at + n] = x.T
            at += n
    for k, refs in oth:
        b = 2 * ((y + 4 - k) & 3) + 1 - core
        at = 0
        for ref in refs:
            n = ref.shape[0]
            x = ref[...]
            _, s = silu_parts(mm(x, wg[:, E : 3 * E]))
            s = s.astype(BF16)
            sk[b, at : at + n] = s[:, :E]
            sv[b, at : at + n] = s[:, E:]
            nt[b, :, at : at + n] = x.T
            at += n
    first = core == 0
    mine = wg[:, 3 * E :]
    other = wo_half[...]
    w_u = jnp.where(first, mine, other)
    w_out[...] = jnp.where(first, other, mine)
    act, slope = silu_parts(mm(n0[...], w_u))
    u[...] = act.astype(BF16)
    su[...] = slope.astype(BF16)
    placing = (lax.broadcasted_iota(I32, (R, T), 0) == ints[0:1, :]).astype(BF16)
    ev_t[...] = mm(placing, events[...], TN)
    pid = jnp.broadcast_to(ints[1:2, :], (T, T)).astype(F32).T.astype(I32)
    pid = jnp.concatenate([pid, pid], axis=1)
    selector = (lax.broadcasted_iota(I32, (T, 2 * T), 1) == pid).astype(F32)
    embedded = mm(selector, table[...], precision=HIGHEST)
    bias_pre = mm(embedded, bias_w1[...], precision=HIGHEST)
    emb[...] = embedded
    bpre[...] = bias_pre
    hid, _ = silu_parts(bias_pre)
    obs[...] = jnp.broadcast_to(jnp.sum(hid * bias_w2[...], axis=1, keepdims=True), (T, E))


def middle_kernel(
    meta, r0, r1, r2, r3, u, su, w_out, ev_t, obs, ints, upstream, head_w1, head_w2,
    d0, d1, d2, d3, gated_o, dout_o, dpre_o, picked_o, dhid_o, act_o, drel_o, dobs_o,
    att,
):
    y = meta[0]
    for k, ref in enumerate((r0, r1, r2, r3)):
        h = (y + 4 - k) & 3
        att[:, pl.ds(pl.multiple_of(h * E, E), E)] = ref[...].astype(F32)
    x = att[...]
    mean = jnp.mean(x, axis=-1, keepdims=True)
    cen = x - mean
    inv = lax.rsqrt(jnp.mean(cen * cen, axis=-1, keepdims=True) + EPSILON)
    normed = cen * inv
    gate = u[...].astype(F32)
    gated = (normed * gate).astype(BF16)
    gated_o[...] = gated
    placing = (lax.broadcasted_iota(I32, (R, T), 0) == ints[0:1, :]).astype(BF16)
    gated_t = mm(placing, gated, TN).astype(BF16)
    picked = (mm(gated_t, w_out[...]) + ev_t[...]).astype(BF16)
    picked_o[...] = picked
    hidden = mm(picked, head_w1[...])
    active, slope = silu_parts(hidden)
    act_o[...] = active
    w2 = head_w2[...]
    relevance = jnp.sum(active * w2, axis=1, keepdims=True)
    observe = obs[:, :1]
    clicked = jnp.broadcast_to(ints[2:3, :], (T, T)).astype(F32).T[:, :1]
    rel_sig = jax.nn.sigmoid(relevance)
    obs_sig = jax.nn.sigmoid(observe)
    missing = jax.nn.sigmoid(-relevance) + rel_sig * jax.nn.sigmoid(-observe)
    d_rel = clicked * (rel_sig - 1.0) + (1.0 - clicked) * rel_sig * (1.0 - rel_sig) * obs_sig / missing
    d_obs = clicked * (obs_sig - 1.0) + (1.0 - clicked) * rel_sig * obs_sig * (1.0 - obs_sig) / missing
    drel_o[...] = jnp.broadcast_to(d_rel, (T, E))
    dobs_o[...] = jnp.broadcast_to(d_obs, (T, E))
    d_hidden = (d_rel * w2 * slope).astype(BF16)
    dhid_o[...] = d_hidden
    d_picked = mm(d_hidden, head_w1[...], NT).astype(BF16)
    d_out = (upstream[...].astype(F32) + mm(placing, d_picked)).astype(BF16)
    dout_o[...] = d_out
    d_gated = mm(d_out, w_out[...], NT)
    dpre_o[...] = (d_gated * normed * su[...].astype(F32)).astype(BF16)
    g = d_gated * gate
    first = jnp.mean(g, axis=-1, keepdims=True)
    second = jnp.mean(g * normed, axis=-1, keepdims=True)
    att[...] = inv * (g - first - normed * second)
    for k, ref in enumerate((d0, d1, d2, d3)):
        h = (y + k) & 3
        ref[...] = att[:, pl.ds(pl.multiple_of(h * E, E), E)].astype(BF16)


def packed(left, right):
    low = (lax.broadcasted_iota(I32, left.shape, 0) & 7) < 4
    n = left.shape[0]
    return jnp.where(low, left, pltpu.roll(right, 4, 0)), jnp.where(low, pltpu.roll(left, n - 4, 0), right)


def grads_kernel(
    meta, nt_own, dpre, gated, d_out, picked, d_hid, active, d_rel, d_obs, ints, emb, bpre, bias_w1, bias_w2,
    x_own, x_oth, s_own, s_oth,
):
    first = meta[1] == 0

    def put(own_ref, oth_ref, col, left, right):
        x_0, x_1 = packed(left, right)
        cols = slice(col, col + left.shape[1])
        own_ref[:, cols] = jnp.where(first, x_0, x_1).astype(BF16)
        oth_ref[:, cols] = jnp.where(first, x_1, x_0).astype(BF16)

    g_u = mm(nt_own[0], dpre[...])
    put(x_own, x_oth, 0, g_u[:, :256], g_u[:, 256:])
    g_wo = mm(gated[...], d_out[...], TN)
    put(x_own, x_oth, 256, g_wo[:, :256], g_wo[:, 256:])
    g_h1 = mm(picked[...], d_hid[...], TN)
    put(x_own, x_oth, 512, g_h1[:, :128], g_h1[:, 128:])
    hid, slope = silu_parts(bpre[...])
    d_bias = d_obs[...] * bias_w2[...] * slope
    g_b1 = mm(emb[...], d_bias, TN, HIGHEST)
    d_emb = mm(d_bias, bias_w1[...], NT, HIGHEST)
    pid = jnp.broadcast_to(ints[1:2, :], (2 * T, T))
    select_t = (lax.broadcasted_iota(I32, (2 * T, T), 0) == pid).astype(F32)
    g_tab = mm(select_t, d_emb, precision=HIGHEST)
    h2 = mm(active[...], d_rel[...], TN, HIGHEST)
    b2 = mm(hid, d_obs[...], TN, HIGHEST)
    lane2 = lax.broadcasted_iota(I32, (2 * T, E), 1)
    row2 = lax.broadcasted_iota(I32, (2 * T, E), 0)
    h2 = jnp.where(lane2 == (row2 & 1), h2, 0.0)
    b2 = jnp.where(lax.broadcasted_iota(I32, (T, E), 1) == 2, b2, 0.0)
    o2 = lax.broadcasted_iota(I32, (R, 2 * T), 0)
    i2 = lax.broadcasted_iota(I32, (R, 2 * T), 1)
    o1 = lax.broadcasted_iota(I32, (R, T), 0)
    i1 = lax.broadcasted_iota(I32, (R, T), 1)
    parts = []
    for cc in range(2):
        dest2 = 2 * (o2 >> 3) + cc
        dest1 = 2 * (o1 >> 3) + cc
        p_tab = (((o2 & 7) == 4) & (i2 == 2 * dest2)) | (((o2 & 7) == 5) & (i2 == 2 * dest2 + 1))
        p_h2 = ((o2 & 7) == 7) & ((i2 >> 1) == dest2)
        p_b1 = ((o1 & 7) == 6) & (i1 == dest1)
        p_b2 = ((o1 & 7) == 7) & (i1 == dest1)
        parts.append(
            mm(p_tab.astype(BF16), g_tab.astype(BF16))
            + mm(p_h2.astype(BF16), h2.astype(BF16))
            + mm(p_b1.astype(BF16), g_b1.astype(BF16))
            + mm(p_b2.astype(BF16), b2.astype(BF16))
        )
    s_own[...] = jnp.where(first, parts[0], parts[1]).astype(BF16)
    s_oth[...] = jnp.where(first, parts[1], parts[0]).astype(BF16)


def backward_kernel(
    meta, q_s, k_s, v_s, r0, r1, r2, r3, sq, sk, sv, nt, s_own, s_oth,
    x_own, x_oth,
    dq_s, dk_s, dv_s,
):
    y, core = meta[0], meta[1]
    dk_s[...] = jnp.zeros_like(dk_s)
    dv_s[...] = jnp.zeros_like(dv_s)
    rows = lax.broadcasted_iota(I32, (R, 1), 0)
    lanes = lax.broadcasted_iota(I32, (1, R), 1)
    for k, ref in enumerate((r0, r1, r2, r3)):
        blk = (y + 4 - k) & 3
        c = 2 * blk + core
        q = q_s[blk]
        g = ref[...]
        pos = lanes + c * R
        start = user_start(pos, meta)

        def step(b, dq):
            key_pos = rows + b * R
            kb = k_s[b]
            h = mm(kb, q, NT) * HALF
            dp = mm(v_s[b], g, NT)
            t = jnp.tanh(h)
            a = 1.0 + t
            w = h * a
            d = dp * (a + w * (1.0 - t))
            keep = (key_pos >= start) & (key_pos <= pos)
            w = jnp.where(keep, w, 0.0).astype(BF16)
            d = jnp.where(keep, d, 0.0).astype(BF16)
            dv_s[b] += mm(w, g)
            dk_s[b] += mm(d, q)
            return dq + mm(d, kb, TN)

        lo = user_start(c * R, meta) // R
        dq_s[blk] = lax.fori_loop(lo, c + 1, step, jnp.zeros((R, E), F32))
    g_q = jnp.zeros((W, E), F32)
    g_k = jnp.zeros((W, E), F32)
    g_v = jnp.zeros((W, E), F32)
    for i in range(4):
        b = 2 * i + core
        d = (dq_s[i] * HALF * sq[i].astype(F32)).astype(BF16)
        g_q = g_q + mm(nt[b], d)
    for b in range(8):
        d = (dk_s[b] * HALF * sk[b].astype(F32)).astype(BF16)
        g_k = g_k + mm(nt[b], d)
        d = (dv_s[b] * sv[b].astype(F32)).astype(BF16)
        g_v = g_v + mm(nt[b], d)
    first = core == 0
    low = (lax.broadcasted_iota(I32, (W, E), 0) & 7) < 4
    x_0, x_1 = packed(g_q, g_k)
    x_own[:, :E] = jnp.where(first, x_0, x_1).astype(BF16)
    x_oth[:, :E] = jnp.where(first, x_1, x_0).astype(BF16)
    v_1 = pltpu.roll(g_v, W - 4, 0)
    x_own[:, E:] = jnp.where(low, jnp.where(first, g_v, v_1), s_own[...].astype(F32)).astype(BF16)
    x_oth[:, E:] = jnp.where(low, jnp.where(first, v_1, g_v), s_oth[...].astype(F32)).astype(BF16)


def sum_kernel(x_ref, g_in, g_out, g_h1, g_small):
    total = None
    for h in range(HEADS):
        part = jnp.zeros((8, 7 * E), F32)
        for i in range(16):
            at = (h * 16 + i) * 8
            part = part + x_ref[at : at + 8, :].astype(F32)
        g_in[:, W + h * E : W + (h + 1) * E] = part[0:4, 6 * E :]
        g_in[:, 2 * W + h * E : 2 * W + (h + 1) * E] = part[0:4, 5 * E : 6 * E]
        g_in[:, 3 * W + h * E : 3 * W + (h + 1) * E] = part[4:8, 5 * E : 6 * E]
        total = part if total is None else total + part
    g_in[:, 0:256] = total[0:4, 0:256]
    g_in[:, 256:512] = total[4:8, 0:256]
    g_out[:, 0:256] = total[0:4, 256:512]
    g_out[:, 256:512] = total[4:8, 256:512]
    g_h1[:, 0:128] = total[0:4, 512:640]
    g_h1[:, 128:256] = total[4:8, 512:640]
    g_small[...] = total[4:8, 768:896]


CHIPS = ("y", "xh", "xl", "z")
SWAP = []
for _i in range(32):
    _xh, _rest, _core = _i // 16, (_i // 2) % 8, _i % 2
    SWAP.append((_i, _i if _xh == _core else (1 - _xh) * 16 + _rest * 2 + 1 - _core))


def swapped(x):
    return lax.ppermute(x, ("xh", "xl", "z", "core"), SWAP)


def across(x):
    return lax.ppermute(x, "core", [(0, 1), (1, 0)])


def ring(x, k):
    return lax.ppermute(x, "y", [(i, (i + k) % 4) for i in range(4)])


def body(
    events, lengths, target_rows, position_ids, labels, upstream,
    w_in, w_out, head_w1, head_w2, table, bias_w1, bias_w2,
):
    y, core = lax.axis_index("y"), lax.axis_index("core")
    w_rows = jnp.concatenate([w_in, w_out], axis=1)
    w_other = across(w_rows)
    w_rows = jnp.where(
        core == 0, jnp.concatenate([w_rows, w_other], axis=0), jnp.concatenate([w_other, w_rows], axis=0)
    )
    shared = jnp.where(core == 0, w_rows[:, :W], w_rows[:, 4 * W :])
    sent = jnp.stack(
        [
            jnp.concatenate(
                [
                    w_rows[:, 2 * W + h * E : 2 * W + (h + 1) * E],
                    w_rows[:, 3 * W + h * E : 3 * W + (h + 1) * E],
                    w_rows[:, W + h * E : W + (h + 1) * E],
                    shared,
                ],
                axis=1,
            )
            for h in range(HEADS)
        ]
    )
    sent = jnp.broadcast_to(sent[:, None], (4, 16, 8, 7 * E)).reshape(W, 7 * E)
    wg = lax.all_to_all(sent, CHIPS, 0, 0, tiled=True)
    w_half = across(wg[:, 3 * E :])

    ev = swapped(events[0])
    ints = swapped(
        jnp.concatenate([target_rows, position_ids, labels, jnp.pad(lengths, ((0, 0), (0, T - 4)))], axis=0)
    )
    meta = jnp.concatenate([jnp.stack([y, core]).astype(I32), ints[3, :6]])
    (n0,) = call(norm_kernel, [sds((R, W), BF16)], [ev], n_smem=0, name="norm")
    n1 = ring(n0, 1)
    n3 = ring(n0, 3)
    n2a = ring(n1[: R // 2], 1)
    n2b = ring(n3[R // 2 :], 3)
    parts = [n0, n1, n3, n2a, n2b]
    parts = parts + [across(p) for p in parts]
    up = swapped(upstream[0])

    qkv = [sds((4, R, E), BF16), sds((8, R, E), BF16), sds((8, R, E), BF16)]
    a0, a1, a2, a3, q_s, k_s, v_s = call(
        forward_kernel, [sds((R, E), BF16)] * 4 + qkv, [meta] + parts + [wg], flops=5 * 10**9, name="forward"
    )
    r1, r2, r3 = ring(a1, 1), ring(a2, 2), ring(a3, 3)
    sq, sk, sv, nt, u, su, w_o, ev_t, emb, bpre, obs = call(
        side_kernel,
        qkv
        + [sds((8, W, R), BF16)]
        + [sds((R, W), BF16)] * 3
        + [sds((T, W), F32)]
        + [sds((T, E), F32)] * 3,
        [meta] + parts + [wg, w_half, ev, ints, table, bias_w1, bias_w2.reshape(1, E)],
        flops=2 * 10**9,
        limit=48,
        name="side",
    )
    w2 = head_w2.reshape(1, 2 * E)
    b2 = bias_w2.reshape(1, E)
    d0, d1, d2, d3, gated, d_out, dpre, picked, d_hid, active, d_rel, d_obs = call(
        middle_kernel,
        [sds((R, E), BF16)] * 4
        + [sds((R, W), BF16)] * 3
        + [sds((T, W), BF16), sds((T, 2 * E), BF16), sds((T, 2 * E), F32), sds((T, E), F32), sds((T, E), F32)],
        [meta, a0, r1, r2, r3, u, su, w_o, ev_t, obs, ints, up, head_w1, w2],
        scratch=[pltpu.VMEM((R, W), F32)],
        flops=10**9,
        name="middle",
    )
    g1, g2, g3 = ring(d1, 1), ring(d2, 2), ring(d3, 3)
    nt_own = lax.dynamic_slice_in_dim(nt, 2 * y + core, 1, 0)
    early, early_oth, s_own, s_oth = call(
        grads_kernel,
        [sds((R, 5 * E), BF16)] * 2 + [sds((R, E), BF16)] * 2,
        [meta, nt_own, dpre, gated, d_out, picked, d_hid, active, d_rel, d_obs, ints, emb, bpre, bias_w1, b2],
        flops=2 * 10**9,
        name="grads",
    )
    early_in = across(early_oth)
    late, late_oth = call(
        backward_kernel,
        [sds((R, 2 * E), BF16)] * 2,
        [meta, q_s, k_s, v_s, d0, g1, g2, g3, sq, sk, sv, nt, s_own, s_oth],
        scratch=[pltpu.VMEM((4, R, E), F32), pltpu.VMEM((8, R, E), F32), pltpu.VMEM((8, R, E), F32)],
        flops=10**10,
        limit=48,
        name="backward",
    )
    late_in = across(late_oth)
    pair = jnp.concatenate(
        [
            (early.astype(F32) + early_in.astype(F32)).astype(BF16),
            (late.astype(F32) + late_in.astype(F32)).astype(BF16),
        ],
        axis=1,
    )
    got = lax.all_to_all(pair, CHIPS, 0, 0, tiled=True)
    g_in, g_out, g_h1, g_small = call(
        sum_kernel,
        [sds((4, 4 * W), F32), sds((4, W), F32), sds((4, 2 * E), F32), sds((4, E), F32)],
        [got],
        n_smem=0,
        name="total",
    )
    return g_in, g_out, g_h1, g_small[3, 0:2], g_small[0:2], g_small[2:3], g_small[3, 2:3]


def solution(mesh):
    fine = Mesh(mesh.devices.reshape(4, 2, 2, 4, 2), ("y", "xh", "xl", "z", "core"))
    ctx, dp = ("y", "xh"), ("xl", "z", "core")
    every = ctx + dp
    in_specs = (
        P(dp, ctx, None),
        P(dp, None),
        P(dp, ctx),
        P(dp, ctx),
        P(dp, ctx),
        P(dp, ctx, None),
        P(every, None),
        P(every, None),
        P(),
        P(),
        P(),
        P(),
        P(),
    )
    out_specs = (
        P(every, None),
        P(every, None),
        P(every, None),
        P(every),
        P(every, None),
        P(every, None),
        P(every),
    )
    return jax.shard_map(body, mesh=fine, in_specs=in_specs, out_specs=out_specs, check_vma=False)
```

time: 905 us -> 151 us (0.17)
  waiting for transfers between devices: 360 us -> 10.8 us
  local copies, waits for them, and re-layouts: 211 us -> 8.23 us
  matrix products: 163 us -> 0 us
  blocking collectives: 98.8 us -> 27.4 us
  Pallas kernels: 0 us -> 54.7 us
  other arithmetic: 52.1 us -> 1.13 us
  starting transfers between devices: 0.2 us -> 48.4 us
  between operations: 14.3 us -> 0.96 us
    all_gather x3 -> x0, waiting for transfers between devices: 164 us -> none  [the longest x1 68.4 us: body(): lax.all_gather(w_in, ('ctx', 'dp'), axis=0, tiled=True)]
    dot_general x65 -> x0, matrix products: 163 us -> none  [the longest x8 39.4 us: block_weights(): jnp.einsum('rhe,che->hrc', query3, key3, preferred_element_type=jnp.float32)]
    reduce_scatter x1 -> x0, waiting for transfers between devices: 103 us -> none  [body(): lax.psum_scatter(spread.astype(jnp.bfloat16), 'ctx', scatter_dimension=0,...]
    unnamed x6 -> x0, waiting for transfers between devices: 92.3 us -> none
    dynamic_slice x32 -> x1, local copies, waits for them, and re-layouts: 77.2 us -> 1.08 us  [body(): nt_own = lax.dynamic_slice_in_dim(nt, 2 * y + core, 1, 0)]
    unnamed x1 -> x0, blocking collectives: 64.3 us -> none
    pallas_call x0 -> x7, Pallas kernels: none -> 54.7 us  [call(): pl.pallas_call(kernel, out_shape=tuple(outs), in_specs=smem() * n_smem +...]
    mul x8 -> x0, local copies, waits for them, and re-layouts: 42.3 us -> none  [silu_slope(): return sigmoid_value * (1.0 + argument * (1.0 - sigmoid_value))]
  transfers between devices with their start and end apart: 5 -> 23, of which waited for: 5 -> 5; matrix products, arithmetic and copies ran while one was open for 2% -> 2% of each run, Pallas kernels for 0% -> 33%
where the time goes in v1:
time: 151 us; the launch traced here: 152 us
  Pallas kernels  54.7 us (36%)
  starting transfers between devices  48.4 us (32%)
  blocking collectives  27.4 us (18%)
  waiting for transfers between devices  10.8 us (7%)
  local copies, waits for them, and re-layouts  8.23 us (5%)
    pallas_call x7, Pallas kernels, call(): pl.pallas_call(kernel, out_shape=tuple(outs), in_specs=smem() * n_smem +...  54.7 us
    all_to_all x1, blocking collectives, body(): got = lax.all_to_all(pair, CHIPS, 0, 0, tiled=True)  27.4 us
    all_to_all x1, starting transfers between devices, body(): wg = lax.all_to_all(sent, CHIPS, 0, 0, tiled=True)  21.9 us
    ppermute x10, starting transfers between devices, ring(): return lax.ppermute(x, 'y', [(i, (i + k) % 4) for i in range(4)])  15.2 us
    ppermute x10, waiting for transfers between devices, ring(): return lax.ppermute(x, 'y', [(i, (i + k) % 4) for i in range(4)])  9.21 us
    ppermute x9, starting transfers between devices, across(): return lax.ppermute(x, 'core', [(0, 1), (1, 0)])  7.18 us
    ppermute x3, starting transfers between devices, swapped(): return lax.ppermute(x, ('xh', 'xl', 'z', 'core'), SWAP)  4.17 us
  transfers between devices with their start and end apart: 23, of which 5 were waited for; matrix products, arithmetic and copies ran while one was open for 2% of the time, Pallas kernels for 33%

profile of v1, /device:TPU:0, one launch (start us, length us, event | category | flops | bytes accessed | tf_op | source)
XLA Modules:
  0.0 151.6 jit_solution(5998693007102279014)
XLA Ops:
  0.6 0.7 constant_dynamic-update-slice_fusion.1
  1.4 0.7 constant_dynamic-update-slice_fusion
  2.1 1.7 %collective-permute-start.1 = (bf16[512,512]{1,0:T(8,128)(2,1)}, bf16[512,512]{1,0:T(8,128)(2,1)S(1)}, u32[]{:S(2)}, u32[]{:S(2)}) collective-permute-start(bf16[512,512]{1,0:T(8,128)(2,1)} %bitcast.32), channel_id=1, source_target_pairs={{0,0},{1,16},{2,2},{3,18},{4,4},{5,20},{6,6},{7,22},{8,8},{9,24},{... | collective-permute-start | bytes 1572872 | tf_op jit(solution)/shard_map/ppermute | solution.py:385
  4.2 3.2 %collective-permute-start.3 = (bf16[512,512]{1,0:T(8,128)(2,1)S(1)}, bf16[512,512]{1,0:T(8,128)(2,1)S(1)}, u32[]{:S(2)}, u32[]{:S(2)}) collective-permute-start(bf16[512,512]{1,0:T(8,128)(2,1)S(1)} %norm.1.n0), channel_id=1, source_target_pairs={{0,96},{32,0},{64,32},{96,64},{1,97},{33,1},{65,33},{97,65},{2,98}... | collective-permute-start | bytes 1572872 | tf_op jit(solution)/shard_map/ppermute | solution.py:393
  7.4 1.0 broadcast_in_dim.2
  8.4 21.9 %all-to-all-start = ((bf16[64,8,896]{2,1,0:T(8,128)(2,1)}), bf16[64,8,896]{2,1,0:T(8,128)(2,1)S(1)}, u32[]{:S(2)}, u32[]{:S(2)}) async-start(bf16[64,8,896]{2,1,0:T(8,128)(2,1)} %bitcast.31), calls=%async_computation | async-start | bytes 1835008 | tf_op jit(solution)/shard_map/all_to_all | solution.py:422
  30.4 3.1 %collective-permute-start.5 = (bf16[256,512]{1,0:T(8,128)(2,1)S(1)}, bf16[256,512]{1,0:T(8,128)(2,1)S(1)}, u32[]{:S(2)}, u32[]{:S(2)}) collective-permute-start(bf16[256,512]{1,0:T(8,128)(2,1)S(1)} %slice.89), channel_id=1, source_target_pairs={{0,96},{32,0},{64,32},{96,64},{1,97},{33,1},{65,33},{97,65},{2,98}... | collective-permute-start | bytes 786440 | tf_op jit(solution)/shard_map/ppermute | solution.py:393
  33.5 0.7 slice.88
  34.2 0.7 pad_add_fusion
  34.9 0.6 collective-permute-start
  35.6 4.5 %collective-permute-start.7 = (bf16[512,512]{1,0:T(8,128)(2,1)S(1)}, bf16[512,512]{1,0:T(8,128)(2,1)}, u32[]{:S(2)}, u32[]{:S(2)}) collective-permute-start(bf16[512,512]{1,0:T(8,128)(2,1)S(1)} %collective-permute-done.2.n1), channel_id=1, source_target_pairs={{0,1},{1,0},{2,3},{3,2},{4,5},{5,4},{6,7},{7,6},{8,9},{9,8},{10,11... | collective-permute-start | bytes 1572872 | tf_op jit(solution)/shard_map/ppermute | solution.py:389
  40.0 1.9 %collective-permute-start.8 = (bf16[512,512]{1,0:T(8,128)(2,1)S(1)}, bf16[512,512]{1,0:T(8,128)(2,1)}, u32[]{:S(2)}, u32[]{:S(2)}) collective-permute-start(bf16[512,512]{1,0:T(8,128)(2,1)S(1)} %collective-permute-done.3.n3), channel_id=1, source_target_pairs={{0,1},{1,0},{2,3},{3,2},{4,5},{5,4},{6,7},{7,6},{8,9},{9,8},{10,11... | collective-permute-start | bytes 1572872 | tf_op jit(solution)/shard_map/ppermute | solution.py:389
  41.9 4.6 %collective-permute-done.5.n2b = bf16[256,512]{1,0:T(8,128)(2,1)S(1)} collective-permute-done((bf16[256,512]{1,0:T(8,128)(2,1)S(1)}, bf16[256,512]{1,0:T(8,128)(2,1)S(1)}, u32[]{:S(2)}, u32[]{:S(2)}) %collective-permute-start.5) | collective-permute-done | bytes 262176 | tf_op jit(solution)/shard_map/ppermute | solution.py:393
  46.5 2.0 %collective-permute-done.4.n2a = bf16[256,512]{1,0:T(8,128)(2,1)} collective-permute-done((bf16[256,512]{1,0:T(8,128)(2,1)}, bf16[256,512]{1,0:T(8,128)(2,1)}, u32[]{:S(2)}, u32[]{:S(2)}) %collective-permute-start.4) | collective-permute-done | bytes 262176 | tf_op jit(solution)/shard_map/ppermute | solution.py:393
  49.3 1.8 %collective-permute-start.16 = (bf16[512,512]{1,0:T(8,128)(2,1)}, bf16[512,512]{1,0:T(8,128)(2,1)S(1)}, u32[]{:S(2)}, u32[]{:S(2)}) collective-permute-start(bf16[512,512]{1,0:T(8,128)(2,1)} %bitcast.33), channel_id=1, source_target_pairs={{0,0},{1,16},{2,2},{3,18},{4,4},{5,20},{6,6},{7,22},{8,8},{9,24},{... | collective-permute-start | bytes 1572872 | tf_op jit(solution)/shard_map/ppermute | solution.py:385
  51.1 14.3 %forward.1 = (bf16[512,128]{1,0:T(8,128)(2,1)S(1)}, bf16[512,128]{1,0:T(8,128)(2,1)S(1)}, bf16[512,128]{1,0:T(8,128)(2,1)S(1)}, bf16[512,128]{1,0:T(8,128)(2,1)S...) custom-call(s32[8]{0:T(128)S(1)} %pad_add_fusion.1.meta, ...), custom_call_target="tpu_custom_call" | custom-call | flops 5000000000 | bytes 8257568 | tf_op jit(solution)/shard_map/forward/pallas_call | solution.py:58
  65.7 1.9 %collective-permute-start.14 = (bf16[512,128]{1,0:T(8,128)(2,1)S(1)}, bf16[512,128]{1,0:T(8,128)(2,1)S(1)}, u32[]{:S(2)}, u32[]{:S(2)}) collective-permute-start(bf16[512,128]{1,0:T(8,128)(2,1)S(1)} %get-tuple-element.50), channel_id=1, source_target_pairs={{0,64},{32,96},{64,0},{96,32},{1,65},{33,97},{65,1},{97,33},{2,66}... | collective-permute-start | bytes 393224 | tf_op jit(solution)/shard_map/ppermute | solution.py:393
  67.6 1.6 %collective-permute-start.15 = (bf16[512,128]{1,0:T(8,128)(2,1)S(1)}, bf16[512,128]{1,0:T(8,128)(2,1)S(1)}, u32[]{:S(2)}, u32[]{:S(2)}) collective-permute-start(bf16[512,128]{1,0:T(8,128)(2,1)S(1)} %get-tuple-element.51), channel_id=1, source_target_pairs={{0,96},{32,0},{64,32},{96,64},{1,97},{33,1},{65,33},{97,65},{2,98}... | collective-permute-start | bytes 393224 | tf_op jit(solution)/shard_map/ppermute | solution.py:393
  69.2 0.8 copy-done.13
  70.0 0.9 copy-done.4
  70.9 7.5 %side.1 = (bf16[4,512,128]{2,1,0:T(8,128)(2,1)S(1)}, bf16[8,512,128]{2,1,0:T(8,128)(2,1)}, bf16[8,512,128]{2,1,0:T(8,128)(2,1)}, bf16[8,512,512]{2,1,0:T(8,128)(...) custom-call(s32[8]{0:T(128)S(1)} %pad_add_fusion.1.meta, ...), custom_call_target="tpu_custom_call" | custom-call | flops 2000000000 | bytes 15206944 | tf_op jit(solution)/shard_map/side/pallas_call | solution.py:58
  78.5 1.1 constant_dynamic-slice_fusion.nt_own
  79.6 3.0 %middle.1 = (bf16[512,128]{1,0:T(8,128)(2,1)S(1)}, bf16[512,128]{1,0:T(8,128)(2,1)S(1)}, bf16[512,128]{1,0:T(8,128)(2,1)S(1)}, bf16[512,128]{1,0:T(8,128)(2,1)S(...) custom-call(s32[8]{0:T(128)S(1)} %pad_add_fusion.1.meta, ...), custom_call_target="tpu_custom_call" | custom-call | flops 1000000000 | bytes 5770272 | tf_op jit(solution)/shard_map/middle/pallas_call | solution.py:58
  83.1 2.2 %collective-permute-start.19 = (bf16[512,128]{1,0:T(8,128)(2,1)S(1)}, bf16[512,128]{1,0:T(8,128)(2,1)S(1)}, u32[]{:S(2)}, u32[]{:S(2)}) collective-permute-start(bf16[512,128]{1,0:T(8,128)(2,1)S(1)} %get-tuple-element.74), channel_id=1, source_target_pairs={{0,64},{32,96},{64,0},{96,32},{1,65},{33,97},{65,1},{97,33},{2,66}... | collective-permute-start | bytes 393224 | tf_op jit(solution)/shard_map/ppermute | solution.py:393
  85.3 2.5 %collective-permute-start.20 = (bf16[512,128]{1,0:T(8,128)(2,1)S(1)}, bf16[512,128]{1,0:T(8,128)(2,1)S(1)}, u32[]{:S(2)}, u32[]{:S(2)}) collective-permute-start(bf16[512,128]{1,0:T(8,128)(2,1)S(1)} %get-tuple-element.75), channel_id=1, source_target_pairs={{0,96},{32,0},{64,32},{96,64},{1,97},{33,1},{65,33},{97,65},{2,98}... | collective-permute-start | bytes 393224 | tf_op jit(solution)/shard_map/ppermute | solution.py:393
  87.8 2.8 %grads.1 = (bf16[512,640]{1,0:T(8,128)(2,1)S(1)}, bf16[512,640]{1,0:T(8,128)(2,1)S(1)}, bf16[512,128]{1,0:T(8,128)(2,1)S(1)}, bf16[512,128]{1,0:T(8,128)(2,1)S(1)}) custom-call(s32[8]{0:T(128)S(1)} %pad_add_fusion.1.meta, bf16[1,512,512]{2,1,0:T(8,128)(2,1)S(1)} %constant_dynamic-slice_fusion.nt_own, bf16[512,512]{1,0:T(8,128)(2,1)S(1)} %get-tuple-element.57.dpre, ...), custom_call_target="tpu_custom_call" | custom-call | flops 2000000000 | bytes 4327968 | tf_op jit(solution)/shard_map/grads/pallas_call | solution.py:58
  90.7 2.0 %collective-permute-done.18.r1 = bf16[512,128]{1,0:T(8,128)(2,1)S(1)} collective-permute-done((bf16[512,128]{1,0:T(8,128)(2,1)S(1)}, bf16[512,128]{1,0:T(8,128)(2,1)S(1)}, u32[]{:S(2)}, u32[]{:S(2)}) %collective-permute-start.18) | collective-permute-done | bytes 131104 | tf_op jit(solution)/shard_map/ppermute | solution.py:393
  93.3 26.0 %backward.1 = (bf16[512,256]{1,0:T(8,128)(2,1)S(1)}, bf16[512,256]{1,0:T(8,128)(2,1)S(1)}) custom-call(s32[8]{0:T(128)S(1)} %pad_add_fusion.1.meta, bf16[4,512,128]{2,1,0:T(8,128)(2,1)S(1)} %get-tuple-element.69.q_s, bf16[8,512,128]{2,1,0:T(8,128)(2,1)S(1)} %get-tuple-element.70.k_s, bf16[8,512,128]{2,1,0:T(8,128)(2,1)S(1)} %get-tuple-element.71.v_s, ...), custom_call_target="tpu_custom_call" | custom-call | flops 10000000000 | bytes 10747936 | tf_op jit(solution)/shard_map/backward/pallas_call | solution.py:58
  119.4 1.5 %collective-permute-done.21 = bf16[512,256]{1,0:T(8,128)(2,1)S(1)} collective-permute-done((bf16[512,256]{1,0:T(8,128)(2,1)S(1)}, bf16[512,256]{1,0:T(8,128)(2,1)S(1)}, u32[]{:S(2)}, u32[]{:S(2)}) %collective-permute-start.21) | collective-permute-done | bytes 262176 | tf_op jit(solution)/shard_map/ppermute | solution.py:389
  121.3 27.4 %all_to_all.22 = bf16[64,8,896]{2,1,0:T(8,128)(2,1)S(1)} all-to-all(bf16[64,8,896]{2,1,0:T(8,128)(2,1)S(1)} %maximum_bitcast_fusion), channel_id=1, replica_groups=mesh['y'=4,'xh'=2,'xl'=2,'z'=4,'core'=2] {'y','xh','xl','z'}, dimensions={0} | all-to-all | bytes 1835008 | tf_op jit(solution)/shard_map/all_to_all | solution.py:495
  148.7 0.7 total.1
  150.0 0.6 slice.87
  (72 shorter events, 4.7 us)
Async XLA Ops:
  2.1 1.7 %collective-permute-start.11 = (bf16[4,2560]{1,0:T(4,128)(2,1)S(1)}, bf16[4,2560]{1,0:T(4,128)(2,1)S(1)}, u32[]{:S(2)}, u32[]{:S(2)}) collective-permute-start(bf16[4,2560]{1,0:T(4,128)(2,1)S(1)} %constant_dynamic-update-slice_fusion), channel_id=1, source_target_pairs={{0,1},{1,0},{2,3},{3,2},{4,5},{5,4},{6,7},{7,6},{8,9},{9,8},{10,11... | collective-permute-start | bytes 61448 | tf_op jit(solution)/shard_map/ppermute | solution.py:389
  2.1 1.8 %collective-permute-start.1 = (bf16[512,512]{1,0:T(8,128)(2,1)}, bf16[512,512]{1,0:T(8,128)(2,1)S(1)}, u32[]{:S(2)}, u32[]{:S(2)}) collective-permute-start(bf16[512,512]{1,0:T(8,128)(2,1)} %bitcast.32), channel_id=1, source_target_pairs={{0,0},{1,16},{2,2},{3,18},{4,4},{5,20},{6,6},{7,22},{8,8},{9,24},{... | collective-permute-start | bytes 1572872 | tf_op jit(solution)/shard_map/ppermute | solution.py:385
  4.2 26.2 %collective-permute-start.3 = (bf16[512,512]{1,0:T(8,128)(2,1)S(1)}, bf16[512,512]{1,0:T(8,128)(2,1)S(1)}, u32[]{:S(2)}, u32[]{:S(2)}) collective-permute-start(bf16[512,512]{1,0:T(8,128)(2,1)S(1)} %norm.1.n0), channel_id=1, source_target_pairs={{0,96},{32,0},{64,32},{96,64},{1,97},{33,1},{65,33},{97,65},{2,98}... | collective-permute-start | bytes 1572872 | tf_op jit(solution)/shard_map/ppermute | solution.py:393
  7.3 26.2 %collective-permute-start.2 = (bf16[512,512]{1,0:T(8,128)(2,1)S(1)}, bf16[512,512]{1,0:T(8,128)(2,1)S(1)}, u32[]{:S(2)}, u32[]{:S(2)}) collective-permute-start(bf16[512,512]{1,0:T(8,128)(2,1)S(1)} %norm.1.n0), channel_id=1, source_target_pairs={{0,32},{32,64},{64,96},{96,0},{1,33},{33,65},{65,97},{97,1},{2,34}... | collective-permute-start | bytes 1572872 | tf_op jit(solution)/shard_map/ppermute | solution.py:393
  7.4 26.8 %copy-start.10 = (s32[1,4]{1,0:T(1,128)S(1)}, s32[1,4]{1,0:T(1,128)}, u32[]{:S(2)}) copy-start(s32[1,4]{1,0:T(1,128)} %param.14) | copy-start | bytes 52
  7.4 26.8 %copy-start.11 = (s32[1,128]{1,0:T(1,128)S(1)}, s32[1,128]{1,0:T(1,128)}, u32[]{:S(2)}) copy-start(s32[1,128]{1,0:T(1,128)} %param.17) | copy-start | bytes 1540
  7.4 26.8 %copy-start.12 = (s32[1,128]{1,0:T(1,128)S(1)}, s32[1,128]{1,0:T(1,128)}, u32[]{:S(2)}) copy-start(s32[1,128]{1,0:T(1,128)} %param.16) | copy-start | bytes 1540
  8.4 40.1 %all-to-all-start = ((bf16[64,8,896]{2,1,0:T(8,128)(2,1)}), bf16[64,8,896]{2,1,0:T(8,128)(2,1)S(1)}, u32[]{:S(2)}, u32[]{:S(2)}) async-start(bf16[64,8,896]{2,1,0:T(8,128)(2,1)} %bitcast.31), calls=%async_computation | async-start | bytes 1835008 | tf_op jit(solution)/shard_map/all_to_all | solution.py:422
  30.3 18.3 %collective-permute-start.6 = (bf16[512,512]{1,0:T(8,128)(2,1)S(1)}, bf16[512,512]{1,0:T(8,128)(2,1)S(1)}, u32[]{:S(2)}, u32[]{:S(2)}) collective-permute-start(bf16[512,512]{1,0:T(8,128)(2,1)S(1)} %norm.1.n0), channel_id=1, source_target_pairs={{0,1},{1,0},{2,3},{3,2},{4,5},{5,4},{6,7},{7,6},{8,9},{9,8},{10,11... | collective-permute-start | bytes 1572872 | tf_op jit(solution)/shard_map/ppermute | solution.py:389
  30.4 16.1 %collective-permute-start.5 = (bf16[256,512]{1,0:T(8,128)(2,1)S(1)}, bf16[256,512]{1,0:T(8,128)(2,1)S(1)}, u32[]{:S(2)}, u32[]{:S(2)}) collective-permute-start(bf16[256,512]{1,0:T(8,128)(2,1)S(1)} %slice.89), channel_id=1, source_target_pairs={{0,96},{32,0},{64,32},{96,64},{1,97},{33,1},{65,33},{97,65},{2,98}... | collective-permute-start | bytes 786440 | tf_op jit(solution)/shard_map/ppermute | solution.py:393
  34.2 14.3 %collective-permute-start.4 = (bf16[256,512]{1,0:T(8,128)(2,1)}, bf16[256,512]{1,0:T(8,128)(2,1)}, u32[]{:S(2)}, u32[]{:S(2)}) collective-permute-start(bf16[256,512]{1,0:T(8,128)(2,1)} %slice.88), channel_id=1, source_target_pairs={{0,32},{32,64},{64,96},{96,0},{1,33},{33,65},{65,97},{97,1},{2,34}... | collective-permute-start | bytes 786440 | tf_op jit(solution)/shard_map/ppermute | solution.py:393
  34.9 5.1 %collective-permute-start = (s32[4,128]{1,0:T(4,128)S(1)}, s32[4,128]{1,0:T(4,128)S(1)}, u32[]{:S(2)}, u32[]{:S(2)}) collective-permute-start(s32[4,128]{1,0:T(4,128)S(1)} %pad_add_fusion), channel_id=1, source_target_pairs={{0,0},{1,16},{2,2},{3,18},{4,4},{5,20},{6,6},{7,22},{8,8},{9,24},{... | collective-permute-start | bytes 6152 | tf_op jit(solution)/shard_map/ppermute | solution.py:385
  35.6 13.7 %collective-permute-start.7 = (bf16[512,512]{1,0:T(8,128)(2,1)S(1)}, bf16[512,512]{1,0:T(8,128)(2,1)}, u32[]{:S(2)}, u32[]{:S(2)}) collective-permute-start(bf16[512,512]{1,0:T(8,128)(2,1)S(1)} %collective-permute-done.2.n1), channel_id=1, source_target_pairs={{0,1},{1,0},{2,3},{3,2},{4,5},{5,4},{6,7},{7,6},{8,9},{9,8},{10,11... | collective-permute-start | bytes 1572872 | tf_op jit(solution)/shard_map/ppermute | solution.py:389
  40.0 11.1 %collective-permute-start.8 = (bf16[512,512]{1,0:T(8,128)(2,1)S(1)}, bf16[512,512]{1,0:T(8,128)(2,1)}, u32[]{:S(2)}, u32[]{:S(2)}) collective-permute-start(bf16[512,512]{1,0:T(8,128)(2,1)S(1)} %collective-permute-done.3.n3), channel_id=1, source_target_pairs={{0,1},{1,0},{2,3},{3,2},{4,5},{5,4},{6,7},{7,6},{8,9},{9,8},{10,11... | collective-permute-start | bytes 1572872 | tf_op jit(solution)/shard_map/ppermute | solution.py:389
  46.5 19.0 %copy-start.3 = (bf16[256,512]{1,0:T(8,128)(2,1)}, bf16[256,512]{1,0:T(8,128)(2,1)S(1)}, u32[]{:S(2)}) copy-start(bf16[256,512]{1,0:T(8,128)(2,1)S(1)} %collective-permute-done.5.n2b) | copy-start | bytes 786436
  46.5 4.6 %collective-permute-start.10 = (bf16[256,512]{1,0:T(8,128)(2,1)S(1)}, bf16[256,512]{1,0:T(8,128)(2,1)}, u32[]{:S(2)}, u32[]{:S(2)}) collective-permute-start(bf16[256,512]{1,0:T(8,128)(2,1)S(1)} %collective-permute-done.5.n2b), channel_id=1, source_target_pairs={{0,1},{1,0},{2,3},{3,2},{4,5},{5,4},{6,7},{7,6},{8,9},{9,8},{10,11... | collective-permute-start | bytes 786440 | tf_op jit(solution)/shard_map/ppermute | solution.py:389
  48.5 2.6 %collective-permute-start.9 = (bf16[256,512]{1,0:T(8,128)(2,1)}, bf16[256,512]{1,0:T(8,128)(2,1)}, u32[]{:S(2)}, u32[]{:S(2)}) collective-permute-start(bf16[256,512]{1,0:T(8,128)(2,1)} %collective-permute-done.4.n2a), channel_id=1, source_target_pairs={{0,1},{1,0},{2,3},{3,2},{4,5},{5,4},{6,7},{7,6},{8,9},{9,8},{10,11... | collective-permute-start | bytes 786440 | tf_op jit(solution)/shard_map/ppermute | solution.py:389
  48.6 17.0 %copy-start = (bf16[64,8,896]{2,1,0:T(8,128)(2,1)}, bf16[64,8,896]{2,1,0:T(8,128)(2,1)S(1)}, u32[]{:S(2)}) copy-start(bf16[64,8,896]{2,1,0:T(8,128)(2,1)S(1)} %all-to-all-done) | copy-start | bytes 2752516
  48.6 20.6 %collective-permute-start.12 = (bf16[512,512]{1,0:T(8,128)(2,1)S(1)}, bf16[512,512]{1,0:T(8,128)(2,1)S(1)}, u32[]{:S(2)}, u32[]{:S(2)}) collective-permute-start(bf16[512,512]{1,0:T(8,128)(2,1)S(1)} %slice.104), channel_id=1, source_target_pairs={{0,1},{1,0},{2,3},{3,2},{4,5},{5,4},{6,7},{7,6},{8,9},{9,8},{10,11... | collective-permute-start | bytes 1572872 | tf_op jit(solution)/shard_map/ppermute | solution.py:389
  49.3 20.7 %copy-start.5 = (f32[256,128]{1,0:T(8,128)S(1)}, f32[256,128]{1,0:T(8,128)}, u32[]{:S(2)}) copy-start(f32[256,128]{1,0:T(8,128)} %table.1) | copy-start | bytes 393220
  49.3 20.7 %copy-start.6 = (f32[128,128]{1,0:T(8,128)S(1)}, f32[128,128]{1,0:T(8,128)}, u32[]{:S(2)}) copy-start(f32[128,128]{1,0:T(8,128)} %bias_w1.3) | copy-start | bytes 196612
  49.3 20.7 %copy-start.8 = (f32[128]{0:T(128)S(1)}, f32[128]{0:T(128)}, u32[]{:S(2)}) copy-start(f32[128]{0:T(128)} %param.25) | copy-start | bytes 1540
  49.3 30.2 %collective-permute-start.16 = (bf16[512,512]{1,0:T(8,128)(2,1)}, bf16[512,512]{1,0:T(8,128)(2,1)S(1)}, u32[]{:S(2)}, u32[]{:S(2)}) collective-permute-start(bf16[512,512]{1,0:T(8,128)(2,1)} %bitcast.33), channel_id=1, source_target_pairs={{0,0},{1,16},{2,2},{3,18},{4,4},{5,20},{6,6},{7,22},{8,8},{9,24},{... | collective-permute-start | bytes 1572872 | tf_op jit(solution)/shard_map/ppermute | solution.py:385
  65.5 14.0 %collective-permute-start.13 = (bf16[512,128]{1,0:T(8,128)(2,1)S(1)}, bf16[512,128]{1,0:T(8,128)(2,1)S(1)}, u32[]{:S(2)}, u32[]{:S(2)}) collective-permute-start(bf16[512,128]{1,0:T(8,128)(2,1)S(1)} %get-tuple-element.49), channel_id=1, source_target_pairs={{0,32},{32,64},{64,96},{96,0},{1,33},{33,65},{65,97},{97,1},{2,34}... | collective-permute-start | bytes 393224 | tf_op jit(solution)/shard_map/ppermute | solution.py:393
  65.7 13.9 %collective-permute-start.14 = (bf16[512,128]{1,0:T(8,128)(2,1)S(1)}, bf16[512,128]{1,0:T(8,128)(2,1)S(1)}, u32[]{:S(2)}, u32[]{:S(2)}) collective-permute-start(bf16[512,128]{1,0:T(8,128)(2,1)S(1)} %get-tuple-element.50), channel_id=1, source_target_pairs={{0,64},{32,96},{64,0},{96,32},{1,65},{33,97},{65,1},{97,33},{2,66}... | collective-permute-start | bytes 393224 | tf_op jit(solution)/shard_map/ppermute | solution.py:393
  67.6 12.0 %collective-permute-start.15 = (bf16[512,128]{1,0:T(8,128)(2,1)S(1)}, bf16[512,128]{1,0:T(8,128)(2,1)S(1)}, u32[]{:S(2)}, u32[]{:S(2)}) collective-permute-start(bf16[512,128]{1,0:T(8,128)(2,1)S(1)} %get-tuple-element.51), channel_id=1, source_target_pairs={{0,96},{32,0},{64,32},{96,64},{1,97},{33,1},{65,33},{97,65},{2,98}... | collective-permute-start | bytes 393224 | tf_op jit(solution)/shard_map/ppermute | solution.py:393
  70.9 8.7 %copy-start.7 = (f32[256]{0:T(256)S(1)}, f32[256]{0:T(256)}, u32[]{:S(2)}) copy-start(f32[256]{0:T(256)} %param.22) | copy-start | bytes 3076
  82.6 10.1 %collective-permute-start.18 = (bf16[512,128]{1,0:T(8,128)(2,1)S(1)}, bf16[512,128]{1,0:T(8,128)(2,1)S(1)}, u32[]{:S(2)}, u32[]{:S(2)}) collective-permute-start(bf16[512,128]{1,0:T(8,128)(2,1)S(1)} %get-tuple-element.73), channel_id=1, source_target_pairs={{0,32},{32,64},{64,96},{96,0},{1,33},{33,65},{65,97},{97,1},{2,34}... | collective-permute-start | bytes 393224 | tf_op jit(solution)/shard_map/ppermute | solution.py:393
  83.1 9.6 %collective-permute-start.19 = (bf16[512,128]{1,0:T(8,128)(2,1)S(1)}, bf16[512,128]{1,0:T(8,128)(2,1)S(1)}, u32[]{:S(2)}, u32[]{:S(2)}) collective-permute-start(bf16[512,128]{1,0:T(8,128)(2,1)S(1)} %get-tuple-element.74), channel_id=1, source_target_pairs={{0,64},{32,96},{64,0},{96,32},{1,65},{33,97},{65,1},{97,33},{2,66}... | collective-permute-start | bytes 393224 | tf_op jit(solution)/shard_map/ppermute | solution.py:393
  85.3 8.0 %collective-permute-start.20 = (bf16[512,128]{1,0:T(8,128)(2,1)S(1)}, bf16[512,128]{1,0:T(8,128)(2,1)S(1)}, u32[]{:S(2)}, u32[]{:S(2)}) collective-permute-start(bf16[512,128]{1,0:T(8,128)(2,1)S(1)} %get-tuple-element.75), channel_id=1, source_target_pairs={{0,96},{32,0},{64,32},{96,64},{1,97},{33,1},{65,33},{97,65},{2,98}... | collective-permute-start | bytes 393224 | tf_op jit(solution)/shard_map/ppermute | solution.py:393
  90.6 30.4 %collective-permute-start.17 = (bf16[512,640]{1,0:T(8,128)(2,1)S(1)}, bf16[512,640]{1,0:T(8,128)(2,1)S(1)}, u32[]{:S(2)}, u32[]{:S(2)}) collective-permute-start(bf16[512,640]{1,0:T(8,128)(2,1)S(1)} %get-tuple-element.68), channel_id=1, source_target_pairs={{0,1},{1,0},{2,3},{3,2},{4,5},{5,4},{6,7},{7,6},{8,9},{9,8},{10,11... | collective-permute-start | bytes 1966088 | tf_op jit(solution)/shard_map/ppermute | solution.py:389
  119.3 1.6 %collective-permute-start.21 = (bf16[512,256]{1,0:T(8,128)(2,1)S(1)}, bf16[512,256]{1,0:T(8,128)(2,1)S(1)}, u32[]{:S(2)}, u32[]{:S(2)}) collective-permute-start(bf16[512,256]{1,0:T(8,128)(2,1)S(1)} %get-tuple-element.82), channel_id=1, source_target_pairs={{0,1},{1,0},{2,3},{3,2},{4,5},{5,4},{6,7},{7,6},{8,9},{9,8},{10,11... | collective-permute-start | bytes 786440 | tf_op jit(solution)/shard_map/ppermute | solution.py:389
  (5 other events, 20.4 us)
